TPU v7x, 32 devices: a whole 2x2x4 slice. The times are simulated.
32 devices in a mesh: row: 8 (over z, x), col: 4 (over y, core).
Axes of the slice: x: 2, y: 2, z: 4, core: 2. Of those that a mesh axis runs over, the one named last changes fastest.
Arguments:
- pair: bfloat16 [128, 128, 128], P('row', 'col'), may hold values from -6 to 6
- norm_gain: float32 [128], replicated, may hold values from 0.1 to 1.9
- norm_shift: float32 [128], replicated, may hold values from -3 to 3
- tri_weight: bfloat16 [128, 640], replicated, may hold values from -0.5 to 0.5
- tri_out_gain: float32 [128], replicated, may hold values from 0.1 to 1.9
- tri_out_shift: float32 [128], replicated, may hold values from -3 to 3
- tri_out_weight: bfloat16 [128, 128], replicated, may hold values from -0.5 to 0.5
- att_gain: float32 [128], replicated, may hold values from 0.1 to 1.9
- att_shift: float32 [128], replicated, may hold values from -3 to 3
- att_weight: bfloat16 [128, 512], replicated, may hold values from -0.5 to 0.5
- bias_weight: bfloat16 [128, 4], replicated, may hold values from -12 to 12
- att_out_weight: bfloat16 [128, 128], replicated, may hold values from -0.5 to 0.5
Outputs:
- pair_mid: bfloat16 [128, 128, 128], P('row', 'col')
- pair_out: bfloat16 [128, 128, 128], P('row', 'col')
All inputs are finite; a program needn't handle non-finite values.
Results may differ from a plain program's by a relative error of at most 0.014.
Values may be sent and summed in bfloat16 or wider, within the bound.
A program may use at most 128 MiB of HBM per device.

v0:
```python
import jax
import jax.numpy as jnp
from jax import lax
from jax.sharding import PartitionSpec as P

eps = 1e-05


def normalize(values, gain, shift):
    mean = jnp.mean(values, axis=-1, keepdims=True)
    centred = values - mean
    spread = jnp.mean(centred * centred, axis=-1, keepdims=True)
    return centred * lax.rsqrt(spread + eps) * gain + shift


def local(
    pair,
    norm_gain,
    norm_shift,
    tri_weight,
    tri_out_gain,
    tri_out_shift,
    tri_out_weight,
    att_gain,
    att_shift,
    att_weight,
    bias_weight,
    att_out_weight,
):
    rows_here, cols_here, width = pair.shape
    hidden = tri_out_weight.shape[0]
    heads = bias_weight.shape[1]
    inner = att_out_weight.shape[0]
    head_dim = inner // heads
    normed = normalize(pair.astype(jnp.float32), norm_gain, norm_shift).astype(jnp.bfloat16)
    proj = jnp.dot(normed, tri_weight, preferred_element_type=jnp.float32)
    left = (jax.nn.sigmoid(proj[..., :hidden]) * proj[..., hidden : 2 * hidden]).astype(
        jnp.bfloat16
    )
    right = (
        jax.nn.sigmoid(proj[..., 2 * hidden : 3 * hidden]) * proj[..., 3 * hidden : 4 * hidden]
    ).astype(jnp.bfloat16)
    out_gate = proj[..., 4 * hidden :]
    partial_edges = jnp.einsum(
        "ikh,jkh->ijh",
        left,
        lax.all_gather(right, "row", axis=0, tiled=True),
        preferred_element_type=jnp.float32,
    )
    edges = lax.psum_scatter(partial_edges, "col", scatter_dimension=1, tiled=True)
    tri_normed = normalize(edges, tri_out_gain, tri_out_shift).astype(jnp.bfloat16)
    update = jnp.dot(tri_normed, tri_out_weight, preferred_element_type=jnp.float32)
    pair_mid = (pair.astype(jnp.float32) + jax.nn.sigmoid(out_gate) * update).astype(jnp.bfloat16)
    att_in = normalize(pair_mid.astype(jnp.float32), att_gain, att_shift).astype(jnp.bfloat16)
    proj2 = jnp.dot(att_in, att_weight, preferred_element_type=jnp.float32)
    query = (proj2[..., :inner] * head_dim ** (-0.5)).astype(jnp.bfloat16)
    key = proj2[..., inner : 2 * inner].astype(jnp.bfloat16)
    value = proj2[..., 2 * inner : 3 * inner].astype(jnp.bfloat16)
    att_gate = proj2[..., 3 * inner :]
    local_bias = jnp.einsum(
        "rcd,dh->hrc", att_in, bias_weight, preferred_element_type=jnp.float32
    ).astype(jnp.bfloat16)
    lengthened = lax.all_gather(local_bias, "row", axis=1, tiled=True)
    full_bias = lax.all_gather(lengthened, "col", axis=2, tiled=True)
    first_row = lax.axis_index("row") * rows_here
    queries = query.reshape(rows_here, cols_here, heads, head_dim)
    needed = lax.dynamic_slice_in_dim(full_bias, first_row, rows_here, 2)
    needed = jnp.transpose(needed, (0, 2, 1)).astype(jnp.float32)
    keys_all, values_all = (
        lax.all_gather(key, "row", axis=0, tiled=True),
        lax.all_gather(value, "row", axis=0, tiled=True),
    )
    key_heads = keys_all.reshape(-1, cols_here, heads, head_dim)
    value_heads = values_all.reshape(-1, cols_here, heads, head_dim)
    scores = (
        jnp.einsum("ijhd,kjhd->jhik", queries, key_heads, preferred_element_type=jnp.float32)
        + needed[None]
    )
    top = jnp.max(scores, axis=-1, keepdims=True)
    expd = jnp.exp(scores - top)
    total = jnp.sum(expd, axis=-1)
    mixed = jnp.einsum(
        "jhik,kjhd->ijhd",
        expd.astype(jnp.bfloat16),
        value_heads,
        preferred_element_type=jnp.float32,
    )
    attended = mixed / jnp.transpose(total, (2, 0, 1))[..., None]
    gated = (attended.reshape(rows_here, cols_here, inner) * jax.nn.sigmoid(att_gate)).astype(
        jnp.bfloat16
    )
    pair_out = (
        pair_mid.astype(jnp.float32)
        + jnp.dot(gated, att_out_weight, preferred_element_type=jnp.float32)
    ).astype(jnp.bfloat16)
    return (pair_mid, pair_out)


def solution(mesh):
    return jax.shard_map(
        local,
        mesh=mesh,
        in_specs=(P("row", "col", None), P(), P(), P(), P(), P(), P(), P(), P(), P(), P(), P()),
        out_specs=(P("row", "col", None), P("row", "col", None)),
        check_vma=False,
    )
```

profile of v0, /device:TPU:0, one launch (start us, length us, event | category | flops | bytes accessed | tf_op | source)
XLA Modules:
  0.0 191.3 jit_solution(16954191470215517509)
XLA Ops:
  7.2 0.0 copy-start
  7.2 0.0 all-gather.4.cloned.1.call-start
  7.2 1.1 convert_reduce_fusion.1
  8.3 1.2 fusion.18
  9.5 1.3 fusion.39
  10.8 0.8 fusion.27
  11.6 0.0 all-gather.4.cloned.1.call-update
  11.7 0.0 reduce-scatter.2.cloned.1.call-start
  11.7 0.4 copy.57
  12.1 42.5 %all-gather.4.cloned.1.call-done = bf16[128,32,128]{2,1,0:T(8,128)(2,1)} async-done(((bf16[16,32,128]{2,1,0:T(8,128)(2,1)}), bf16[128,32,128]{2,1,0:T(8,128)(2,1)}) %all-gather.4.cloned.1.call-update) | async-done | bytes 1048592 | tf_op jit(solution)/shard_map/all_gather | solution.py:47
  54.7 7.3 %copy.56 = bf16[128,32,128]{1,0,2:T(8,128)(2,1)} copy(bf16[128,32,128]{2,1,0:T(8,128)(2,1)} %all-gather.4.cloned.1.call-done) | data formatting | bytes 2097152 | tf_op jit(solution)/shard_map/all_gather | solution.py:47
  61.9 4.5 %convolution_bitcast_fusion = f32[16,128,128]{1,0,2:T(8,128)S(1)} fusion(bf16[128,32,128]{1,0,2:T(8,128)(2,1)} %copy.56, bf16[16,32,128]{1,0,2:T(8,128)(2,1)S(1)} %copy.57), kind=kOutput, calls=%fused_computation.1 | convolution fusion | flops 16777216 | bytes 2228224 | tf_op jit(solution)/shard_map/ikh,jkh->ijh/dot_general | solution.py:44
  66.4 0.0 copy-start.11
  66.5 1.6 copy.58
  68.1 0.0 reduce-scatter.2.cloned.1.call-update
  68.1 0.0 all-gather.8.cloned.1.call-start
  68.1 23.7 %reduce-scatter.2.cloned.1.call-done = f32[16,32,128]{2,0,1:T(8,128)} async-done(((f32[16,128,128]{2,0,1:T(8,128)}), f32[16,32,128]{2,0,1:T(8,128)}) %reduce-scatter.2.cloned.1.call-update) | async-done | bytes 262160 | tf_op jit(solution)/shard_map/reduce_scatter | solution.py:50
  91.9 1.1 reduce_sum.65
  93.0 0.1 copy.59
  93.0 0.1 copy.60
  93.1 1.2 multiply_reduce_fusion
  94.3 0.1 copy.61
  94.4 0.1 copy.62
  94.5 1.2 add_convert_fusion
  95.7 0.3 convert_reduce_fusion
  96.0 0.0 copy-start.3
  96.0 0.3 fusion.14
  96.3 0.4 fusion.57
  96.7 0.8 fusion.56
  97.5 0.0 all-gather.8.cloned.1.call-update
  97.5 0.0 all-gather.6.cloned.1.call-start
  97.6 0.5 all-gather.6.cloned.1.call-update
  98.1 0.4 fusion.4
  98.5 30.8 %all_gather.18 = bf16[4,128,32]{2,0,1:T(4,128)(2,1)S(1)} all-gather(bf16[4,16,32]{2,0,1:T(4,128)(2,1)S(1)} %fusion.4), channel_id=1, replica_groups=mesh['row'=8,'col'=4] {'row'}, dimensions={1}, use_global_device_ids=true | all-gather | bytes 36864 | tf_op jit(solution)/shard_map/all_gather | solution.py:63
  129.3 0.1 copy.67
  129.4 5.4 %all_gather.19 = bf16[4,128,128]{1,0,2:T(4,128)(2,1)S(1)} all-gather(bf16[4,128,32]{1,0,2:T(4,128)(2,1)S(1)} %copy.67), channel_id=1, replica_groups=mesh['row'=8,'col'=4] {'col'}, dimensions={2}, use_global_device_ids=true | all-gather | bytes 163840 | tf_op jit(solution)/shard_map/all_gather | solution.py:64
  134.9 0.2 reshape.62
  135.1 2.8 %all-gather.8.cloned.1.call-done = bf16[128,32,128]{2,1,0:T(8,128)(2,1)} async-done(((bf16[16,32,128]{2,1,0:T(8,128)(2,1)}), bf16[128,32,128]{2,1,0:T(8,128)(2,1)}) %all-gather.8.cloned.1.call-update) | async-done | bytes 1048592 | tf_op jit(solution)/shard_map/all_gather | solution.py:70
  138.0 1.9 %copy.65 = bf16[128,32,128]{0,2,1:T(8,128)(2,1)S(1)} copy(bf16[128,32,128]{2,1,0:T(8,128)(2,1)} %all-gather.8.cloned.1.call-done) | data formatting | bytes 2097152 | tf_op jit(solution)/shard_map/all_gather | solution.py:70
  139.9 0.6 fusion.58
  140.6 0.7 fusion.5
  141.3 37.8 %all-gather.6.cloned.1.call-done = bf16[128,32,128]{2,1,0:T(8,128)(2,1)} async-done(((bf16[16,32,128]{2,1,0:T(8,128)(2,1)}), bf16[128,32,128]{2,1,0:T(8,128)(2,1)}) %all-gather.6.cloned.1.call-update) | async-done | bytes 1048592 | tf_op jit(solution)/shard_map/all_gather | solution.py:71
  179.1 1.9 %copy.64 = bf16[128,32,128]{0,2,1:T(8,128)(2,1)S(1)} copy(bf16[128,32,128]{2,1,0:T(8,128)(2,1)} %all-gather.6.cloned.1.call-done) | data formatting | bytes 2097152 | tf_op jit(solution)/shard_map/all_gather | solution.py:71
  181.1 0.0 copy-start.10
  181.1 1.0 fusion
  182.0 0.4 copy.69
  182.5 0.5 reshape.64
  183.0 1.8 fusion.3
  (29 shorter events, 0.1 us)
Async XLA Ops:
  7.2 2.3 %copy-start = (bf16[128,640]{1,0:T(8,128)(2,1)S(1)}, bf16[128,640]{1,0:T(8,128)(2,1)}, u32[]{:S(2)}) copy-start(bf16[128,640]{1,0:T(8,128)(2,1)} %param.15) | copy-start | bytes 491524
  7.2 47.5 %all-gather.4.cloned.1.call-start = ((), (), s32[]{:S(2)}) async-start(), calls=%async_computation.1 | async-start | bytes 1179648 | tf_op jit(solution)/shard_map/all_gather | solution.py:47
  11.7 80.2 %reduce-scatter.2.cloned.1.call-start = ((), (), s32[]{:S(2)}) async-start(), calls=%async_computation.2 | async-start | bytes 1310720 | tf_op jit(solution)/shard_map/reduce_scatter | solution.py:50
  61.9 32.6 %copy-start.5 = (f32[128]{0:T(128)S(1)}, f32[128]{0:T(128)}, u32[]{:S(2)}) copy-start(f32[128]{0:T(128)} %param.17) | copy-start | bytes 1540
  61.9 32.6 %copy-start.6 = (f32[128]{0:T(128)S(1)}, f32[128]{0:T(128)}, u32[]{:S(2)}) copy-start(f32[128]{0:T(128)} %param.16) | copy-start | bytes 1540
  61.9 33.7 %copy-start.2 = (bf16[16,32,128]{2,1,0:T(8,128)(2,1)S(1)}, bf16[16,32,128]{2,1,0:T(8,128)(2,1)}, u32[]{:S(2)}) copy-start(bf16[16,32,128]{2,1,0:T(8,128)(2,1)} %param.12) | copy-start | bytes 393220
  61.9 33.7 %copy-start.9 = (bf16[128,128]{1,0:T(8,128)(2,1)S(1)}, bf16[128,128]{1,0:T(8,128)(2,1)}, u32[]{:S(2)}) copy-start(bf16[128,128]{1,0:T(8,128)(2,1)} %param.18) | copy-start | bytes 98308
  66.4 29.8 %copy-start.4 = (bf16[128,512]{1,0:T(8,128)(2,1)S(1)}, bf16[128,512]{1,0:T(8,128)(2,1)}, u32[]{:S(2)}) copy-start(bf16[128,512]{1,0:T(8,128)(2,1)} %param.21) | copy-start | bytes 393220
  66.4 29.8 %copy-start.7 = (f32[128]{0:T(128)S(1)}, f32[128]{0:T(128)}, u32[]{:S(2)}) copy-start(f32[128]{0:T(128)} %param.20) | copy-start | bytes 1540
  66.4 29.9 %copy-start.8 = (f32[128]{0:T(128)S(1)}, f32[128]{0:T(128)}, u32[]{:S(2)}) copy-start(f32[128]{0:T(128)} %param.19) | copy-start | bytes 1540
  66.4 31.7 %copy-start.11 = (bf16[128,4]{0,1:T(4,128)(2,1)S(1)}, bf16[128,4]{0,1:T(4,128)(2,1)}, u32[]{:S(2)}) copy-start(bf16[128,4]{0,1:T(4,128)(2,1)} %param.22) | copy-start | bytes 3076
  68.1 69.9 %all-gather.8.cloned.1.call-start = ((), (), s32[]{:S(2)}) async-start(), calls=%async_computation.4 | async-start | bytes 1179648 | tf_op jit(solution)/shard_map/all_gather | solution.py:70
  96.0 87.0 %copy-start.3 = (bf16[16,32,128]{2,1,0:T(8,128)(2,1)}, bf16[16,32,128]{2,1,0:T(8,128)(2,1)S(1)}, u32[]{:S(2)}) copy-start(bf16[16,32,128]{2,1,0:T(8,128)(2,1)S(1)} %get-tuple-element.7) | copy-start | bytes 393220
  96.7 43.3 %copy-start.1 = (f32[16,32,512]{2,1,0:T(8,128)}, f32[16,32,512]{2,1,0:T(8,128)S(1)}, u32[]{:S(2)}) copy-start(f32[16,32,512]{2,1,0:T(8,128)S(1)} %get-tuple-element.9) | copy-start | bytes 3145732
  97.5 81.6 %all-gather.6.cloned.1.call-start = ((), (), s32[]{:S(2)}) async-start(), calls=%async_computation.3 | async-start | bytes 1179648 | tf_op jit(solution)/shard_map/all_gather | solution.py:71
  181.1 1.9 copy-start.10
Sparse Core Ops, SparseCore 0:
  11.8 42.8 all-gather.3
  68.2 23.6 reduce-scatter.1
  97.6 40.3 all-gather.7
  140.2 38.8 all-gather.5
where the time goes:
time: 192 us; the launch traced here: 191 us
  waiting for transfers between devices  107 us (56%)
  blocking collectives  36.2 us (19%)
  local copies, waits for them, and re-layouts  15.6 us (8%)
  between operations  14.1 us (7%)
  matrix products  10.2 us (5%)
  other arithmetic  7.53 us (4%)
    all_gather x1, waiting for transfers between devices, local(): lax.all_gather(right, 'row', axis=0, tiled=True)  42.5 us
    all_gather x1, waiting for transfers between devices, local(): lax.all_gather(value, 'row', axis=0, tiled=True)  37.8 us
    all_gather x1, blocking collectives, local(): lengthened = lax.all_gather(local_bias, 'row', axis=1, tiled=True)  30.8 us
    reduce_scatter x1, waiting for transfers between devices, local(): lax.psum_scatter(partial_edges, 'col', scatter_dimension=1, tiled=True)  23.7 us
    all_gather x1, local copies, waits for them, and re-layouts, local(): lax.all_gather(right, 'row', axis=0, tiled=True)  7.27 us
    all_gather x1, blocking collectives, local(): full_bias = lax.all_gather(lengthened, 'col', axis=2, tiled=True)  5.43 us
    dot_general x1, matrix products, local(): jnp.einsum('ikh,jkh->ijh', left, lax.all_gather(right, 'row', axis=0, til...  4.49 us
  transfers between devices with their start and end apart: 4, of which 4 were waited for; matrix products, arithmetic and copies ran while one was open for 2% of the time, Pallas kernels for 0%

commit v1 on v0

v1 whole, which is shorter than its diff:
```python
import functools

import jax
import jax.numpy as jnp
from jax import lax
from jax.experimental import pallas as pl
from jax.experimental.pallas import tpu as pltpu
from jax.sharding import PartitionSpec as P

eps = 1e-05
f32 = jnp.float32
bf16 = jnp.bfloat16
MESH = pl.DeviceIdType.MESH
NT = (((1,), (1,)), ((), ()))
TN = (((0,), (0,)), ((), ()))


def normalize(values, gain, shift):
    mean = jnp.mean(values, axis=-1, keepdims=True)
    centred = values - mean
    spread = jnp.mean(centred * centred, axis=-1, keepdims=True)
    return centred * lax.rsqrt(spread + eps) * gain + shift


def same_group(rows, lanes, row_size, lane_size):
    row = lax.div(lax.broadcasted_iota(jnp.int32, (rows, lanes), 0), jnp.int32(row_size))
    lane = lax.div(lax.broadcasted_iota(jnp.int32, (rows, lanes), 1), jnp.int32(lane_size))
    return row == lane


def kernel(
    R, C,
    pair_ref, ng_ref, ns_ref, tw_ref, tg_ref, ts_ref, tow_ref, ag_ref, as_ref, aw_ref, bw_ref, aow_ref,
    mid_ref, out_ref,
    scr, gate_scr, send_a, recv_a, send_b, recv_b, send_d, recv_d, send_bias, recv_bias, send_f, recv_f,
    ssem_a, rsem_a, ssem_b, rsem_b, ssem_d, rsem_d, ssem_bias, rsem_bias, ssem_f, rsem_f,
):
    D = R * C
    rows, cols, width = pair_ref.shape
    hidden = tow_ref.shape[0]
    heads = bw_ref.shape[1]
    inner = aow_ref.shape[0]
    head_dim = inner // heads
    places = rows * cols
    residues = R * rows
    per = hidden // D
    lanes = per * cols
    share = cols // R
    r, c = lax.axis_index("row"), lax.axis_index("col")
    me = r * C + c

    barrier = pltpu.get_barrier_semaphore()

    def greet(s, _):
        t = lax.rem(me + s, D)
        pl.semaphore_signal(
            barrier, inc=1, device_id=(lax.div(t, C), lax.rem(t, C)), device_id_type=MESH
        )
        return _

    lax.fori_loop(1, D, greet, 0)

    x = pair_ref[...].astype(f32).reshape(places, width)
    normed = normalize(x, ng_ref[...], ns_ref[...]).astype(bf16)

    def spread_channels(side):
        at = 2 * hidden * side
        gate = lax.dot_general(
            tw_ref[:, at : at + hidden], normed, (((0,), (1,)), ((), ())), preferred_element_type=f32
        )
        value = lax.dot_general(
            tw_ref[:, at + hidden : at + 2 * hidden], normed, (((0,), (1,)), ((), ())),
            preferred_element_type=f32,
        )
        turned = jax.nn.sigmoid(gate) * value
        for i in range(rows):
            pieces = [
                turned[h * D : (h + 1) * D, i * cols : (i + 1) * cols] for h in range(per)
            ]
            scr[pl.ds(i, D, stride=rows), :] = jnp.concatenate(pieces, axis=1)
        send_a[:, side] = scr[...].astype(bf16).reshape(D, rows, lanes)

    spread_channels(0)
    spread_channels(1)

    pl.semaphore_wait(barrier, D - 1)

    def copy_a(s, target, source):
        return pltpu.make_async_remote_copy(
            src_ref=send_a.at[target], dst_ref=recv_a.at[lax.rem(source, C), lax.div(source, C)],
            send_sem=ssem_a.at[s], recv_sem=rsem_a.at[s],
            device_id=(lax.div(target, C), lax.rem(target, C)), device_id_type=MESH,
        )

    def copy_b(s, target, source):
        return pltpu.make_async_remote_copy(
            src_ref=send_b.at[lax.rem(target, C), lax.div(target, C)], dst_ref=recv_b.at[source],
            send_sem=ssem_b.at[s], recv_sem=rsem_b.at[s],
            device_id=(lax.div(target, C), lax.rem(target, C)), device_id_type=MESH,
        )

    def copy_bias(s, target, source):
        return pltpu.make_async_remote_copy(
            src_ref=send_bias, dst_ref=recv_bias.at[lax.rem(source, C), lax.div(source, C)],
            send_sem=ssem_bias.at[s], recv_sem=rsem_bias.at[s],
            device_id=(lax.div(target, C), lax.rem(target, C)), device_id_type=MESH,
        )

    def copy_d(s, target, source):
        return pltpu.make_async_remote_copy(
            src_ref=send_d.at[target], dst_ref=recv_d.at[source],
            send_sem=ssem_d.at[s], recv_sem=rsem_d.at[s],
            device_id=(target, c), device_id_type=MESH,
        )

    def copy_f(s, target, source):
        return pltpu.make_async_remote_copy(
            src_ref=send_f.at[target], dst_ref=recv_f.at[source],
            send_sem=ssem_f.at[s], recv_sem=rsem_f.at[s],
            device_id=(target, c), device_id_type=MESH,
        )

    def start_all(copy, here, count):
        def body(s, _):
            copy(s, lax.rem(here + s, count), here).start()
            return _

        lax.fori_loop(1, count, body, 0)

    def arrive_all(copy, here, count):
        def body(s, _):
            copy(s, here, lax.rem(here + count - s, count)).wait_recv()
            return _

        lax.fori_loop(1, count, body, 0)

    def leave_all(copy, here, count):
        def body(s, _):
            copy(s, lax.rem(here + s, count), here).wait_send()
            return _

        lax.fori_loop(1, count, body, 0)

    start_all(copy_a, me, D)
    recv_a[c, r] = send_a[me]
    gate_scr[...] = jax.nn.sigmoid(
        jnp.dot(normed, tw_ref[:, 4 * hidden :], preferred_element_type=f32)
    )
    arrive_all(copy_a, me, D)

    left = jnp.concatenate([recv_a[k, :, 0].reshape(residues, lanes) for k in range(C)], axis=1)
    own_channel = jnp.concatenate([same_group(lanes, lanes, cols, cols)] * C, axis=1)
    for b in range(C):
        block = jnp.concatenate(
            [recv_a[k, :, 1].reshape(residues, lanes)[b * cols : (b + 1) * cols] for k in range(C)],
            axis=1,
        )
        block = jnp.where(own_channel, jnp.concatenate([block] * per, axis=0).astype(f32), 0.0)
        edges = lax.dot_general(left, block.astype(bf16), NT, preferred_element_type=f32)
        send_b[b] = edges.reshape(R, rows, lanes).astype(send_b.dtype)
    start_all(copy_b, me, D)
    recv_b[me] = send_b[c, r]
    arrive_all(copy_b, me, D)

    def over_groups(v):
        total = v
        for h in range(1, per):
            total = total + pltpu.roll(v, h * cols, 1)
        return total

    edges = recv_b[...].astype(f32)
    mean = over_groups(jnp.sum(edges, axis=0)) * (1.0 / hidden)
    centred = edges - mean[None]
    spread = over_groups(jnp.sum(centred * centred, axis=0)) * (1.0 / hidden)
    scaled = centred * lax.rsqrt(spread + eps)[None]
    scr[...] = scaled.reshape(D * rows, lanes)
    gathered = []
    for i in range(rows):
        turned = scr[pl.ds(i, D, stride=rows), :].T
        gathered.append(
            jnp.concatenate([turned[h * cols : (h + 1) * cols] for h in range(per)], axis=1)
        )
    tri_normed = (jnp.concatenate(gathered, axis=0) * tg_ref[...] + ts_ref[...]).astype(bf16)
    update = jnp.dot(tri_normed, tow_ref[...], preferred_element_type=f32)
    x = pair_ref[...].astype(f32).reshape(places, width)
    mid = (x + gate_scr[...] * update).astype(bf16)
    mid_ref[...] = mid.reshape(rows, cols, width)

    att_in = normalize(mid.astype(f32), ag_ref[...], as_ref[...]).astype(bf16).astype(f32)
    for i in range(rows):
        gate_scr[pl.ds(i, cols, stride=rows), :] = att_in[i * cols : (i + 1) * cols]
    att_t = gate_scr[...].astype(bf16)
    send_d[...] = att_t.reshape(R, share, rows, width)
    start_all(copy_d, r, R)
    wide = heads * cols
    spread_bw = jnp.concatenate(
        [
            jnp.broadcast_to(bw_ref[:, h : h + 1].astype(f32), (width, cols))
            for h in range(heads)
        ],
        axis=1,
    ).astype(bf16)
    products = jnp.dot(att_t, spread_bw, preferred_element_type=f32).reshape(cols, rows, wide)
    lane_col = lax.rem(lax.broadcasted_iota(jnp.int32, (rows, wide), 1), jnp.int32(cols))
    bias = jnp.zeros((rows, wide), f32)
    for y in range(cols):
        bias = jnp.where(lane_col == y, products[y], bias)
    send_bias[...] = bias.astype(bf16)
    start_all(copy_bias, me, D)
    recv_d[r] = send_d[r]
    recv_bias[c, r] = send_bias[...]
    arrive_all(copy_d, r, R)

    columns = [recv_d[:, j].reshape(residues, width) for j in range(share)]
    own_head = same_group(wide, inner, cols, head_dim)
    projected = [jnp.dot(a, aw_ref[...], preferred_element_type=f32) for a in columns]
    arrive_all(copy_bias, me, D)
    for j in range(share):
        proj = projected[j]
        query = (proj[:, :inner] * head_dim ** (-0.5)).astype(bf16).astype(f32)
        key = proj[:, inner : 2 * inner].astype(bf16)
        value = proj[:, 2 * inner : 3 * inner].astype(bf16)
        gate = jax.nn.sigmoid(proj[:, 3 * inner :])
        mixed = []
        for b in range(C):
            tiled = jnp.concatenate([query[b * cols : (b + 1) * cols]] * heads, axis=0)
            tiled = jnp.where(own_head, tiled, 0.0).astype(bf16)
            scores = lax.dot_general(key, tiled, NT, preferred_element_type=f32)
            scores = scores + recv_bias[b].reshape(residues, wide).astype(f32)
            top = jnp.max(scores, axis=0, keepdims=True)
            expd = jnp.exp(scores - top)
            total = jnp.sum(expd, axis=0, keepdims=True)
            weights = (expd * (1.0 / total)).astype(bf16)
            full = lax.dot_general(weights, value, TN, preferred_element_type=f32)
            full = jnp.where(own_head, full, 0.0)
            part = full[:cols]
            for h in range(1, heads):
                part = part + full[h * cols : (h + 1) * cols]
            mixed.append(part)
        gated = (jnp.concatenate(mixed, axis=0) * gate).astype(bf16)
        send_f[:, j] = gated.reshape(R, rows, inner)
    start_all(copy_f, r, R)
    recv_f[r] = send_f[r]
    leave_all(copy_a, me, D)
    leave_all(copy_b, me, D)
    leave_all(copy_d, r, R)
    leave_all(copy_bias, me, D)
    arrive_all(copy_f, r, R)
    final = jnp.dot(
        recv_f[...].reshape(places, inner), aow_ref[...], preferred_element_type=f32
    )
    for j in range(cols):
        gate_scr[pl.ds(j, rows, stride=cols), :] = final[j * rows : (j + 1) * rows]
    out = mid_ref[...].astype(f32).reshape(places, width) + gate_scr[...]
    out_ref[...] = out.astype(bf16).reshape(rows, cols, width)
    leave_all(copy_f, r, R)


def local(R, C, pair, ng, ns, tw, tg, ts, tow, ag, ash, aw, bw, aow):
    rows, cols, width = pair.shape
    D = R * C
    hidden = tow.shape[0]
    heads = bw.shape[1]
    inner = aow.shape[0]
    lanes = hidden // D * cols
    share = cols // R
    wide = heads * cols
    places = rows * cols
    vmem = pl.BlockSpec(memory_space=pltpu.VMEM)
    dma = pltpu.SemaphoreType.DMA
    return pl.pallas_call(
        functools.partial(kernel, R, C),
        out_shape=(
            jax.ShapeDtypeStruct(pair.shape, bf16),
            jax.ShapeDtypeStruct(pair.shape, bf16),
        ),
        in_specs=[vmem] * 12,
        out_specs=(vmem, vmem),
        scratch_shapes=[
            pltpu.VMEM((D * rows, lanes), f32),
            pltpu.VMEM((places, width), f32),
            pltpu.VMEM((D, 2, rows, lanes), bf16),
            pltpu.VMEM((C, R, 2, rows, lanes), bf16),
            pltpu.VMEM((C, R, rows, lanes), f32),
            pltpu.VMEM((D, rows, lanes), f32),
            pltpu.VMEM((R, share, rows, width), bf16),
            pltpu.VMEM((R, share, rows, width), bf16),
            pltpu.VMEM((rows, wide), bf16),
            pltpu.VMEM((C, R, rows, wide), bf16),
            pltpu.VMEM((R, share, rows, inner), bf16),
            pltpu.VMEM((R, share, rows, inner), bf16),
            dma((D,)), dma((D,)), dma((D,)), dma((D,)), dma((R,)), dma((R,)),
            dma((D,)), dma((D,)), dma((R,)), dma((R,)),
        ],
        compiler_params=pltpu.CompilerParams(
            collective_id=0, has_side_effects=True, vmem_limit_bytes=48 * 1024 * 1024
        ),
    )(pair, ng[None], ns[None], tw, tg[None], ts[None], tow, ag[None], ash[None], aw, bw, aow)


def solution(mesh):
    R, C = mesh.shape["row"], mesh.shape["col"]
    return jax.shard_map(
        functools.partial(local, R, C),
        mesh=mesh,
        in_specs=(P("row", "col", None), P(), P(), P(), P(), P(), P(), P(), P(), P(), P(), P()),
        out_specs=(P("row", "col", None), P("row", "col", None)),
        check_vma=False,
    )
```

time: 192 us -> 49.5 us (0.26)
  waiting for transfers between devices: 107 us -> 0 us
  Pallas kernels: 0 us -> 42.8 us
  blocking collectives: 36.2 us -> 0 us
  between operations: 14.1 us -> 0.75 us
  matrix products: 10.2 us -> 0 us
  local copies, waits for them, and re-layouts: 15.6 us -> 5.67 us
  other arithmetic: 7.53 us -> 0 us
    all_gather x3 -> x0, waiting for transfers between devices: 83.2 us -> none  [the longest x1 42.5 us: local(): lax.all_gather(right, 'row', axis=0, tiled=True)]
    pallas_call x0 -> x1, Pallas kernels: none -> 42.8 us  [local(): pl.pallas_call(functools.partial(kernel, R, C), out_shape=(jax.ShapeDtype...]
    all_gather x2 -> x0, blocking collectives: 36.2 us -> none  [the longest x1 30.8 us: local(): lengthened = lax.all_gather(local_bias, 'row', axis=1, tiled=True)]
    reduce_scatter x1 -> x0, waiting for transfers between devices: 23.7 us -> none  [local(): lax.psum_scatter(partial_edges, 'col', scatter_dimension=1, tiled=True)]
    all_gather x4 -> x0, local copies, waits for them, and re-layouts: 11.2 us -> none  [the longest x1 7.27 us: local(): lax.all_gather(right, 'row', axis=0, tiled=True)]
    dot_general x8 -> x0, matrix products: 10.2 us -> none  [the longest x1 4.49 us: local(): jnp.einsum('ikh,jkh->ijh', left, lax.all_gather(right, 'row', axis=0, til...]
    unnamed x24 -> x25, local copies, waits for them, and re-layouts: 0.08 us -> 5.67 us
    reduce_sum x6 -> x0, other arithmetic: 5.49 us -> none  [the longest x3 2.61 us: normalize(): spread = jnp.mean(centred * centred, axis=-1, keepdims=True)]
  transfers between devices with their start and end apart: 4 -> 0, of which waited for: 4 -> 0; matrix products, arithmetic and copies ran while one was open for 2% -> 0% of each run, Pallas kernels for 0% -> 0%
where the time goes in v1:
time: 49.5 us; the launch traced here: 49.2 us
  Pallas kernels  42.8 us (86%)
  local copies, waits for them, and re-layouts  5.67 us (11%)
  between operations  0.75 us (2%)
    pallas_call x1, Pallas kernels, local(): pl.pallas_call(functools.partial(kernel, R, C), out_shape=(jax.ShapeDtype...  42.8 us
    unnamed x25, local copies, waits for them, and re-layouts  5.67 us

profile of v1, /device:TPU:0, one launch (start us, length us, event | category | flops | bytes accessed | tf_op | source)
XLA Modules:
  0.0 49.2 jit_solution(3313802960584142072)
XLA Ops:
  0.6 0.0 copy-start.3
  0.6 0.0 copy-start.5
  0.7 0.0 copy-start.6
  0.7 0.0 copy-start.7
  0.7 0.0 copy-start.8
  0.7 0.0 copy-start.9
  0.7 0.0 copy-start.10
  0.7 0.8 %copy.14.bw_ref = bf16[128,4]{1,0:T(8,128)(2,1)S(1)} copy(bf16[128,4]{0,1:T(4,128)(2,1)} %param.22) | data formatting | bytes 2048 | tf_op args[10]
  1.6 0.0 copy-done.3
  1.6 0.0 copy-done.5
  1.6 0.0 copy-done.6
  1.6 0.0 copy-done.7
  1.6 0.0 copy-done.8
  1.6 0.0 copy-done.9
  1.6 0.0 copy-done.10
  1.6 0.0 copy-start
  1.6 0.9 %copy-done = bf16[128,640]{1,0:T(8,128)(2,1)S(1)} copy-done((bf16[128,640]{1,0:T(8,128)(2,1)S(1)}, bf16[128,640]{1,0:T(8,128)(2,1)}, u32[]{:S(2)}) %copy-start) | copy-done | bytes 163864
  2.5 0.0 copy-start.1
  2.5 0.9 %copy-done.1 = bf16[16,32,128]{2,1,0:T(8,128)(2,1)S(1)} copy-done((bf16[16,32,128]{2,1,0:T(8,128)(2,1)S(1)}, bf16[16,32,128]{2,1,0:T(8,128)(2,1)}, u32[]{:S(2)}) %copy-start.1) | copy-done | bytes 131096
  3.4 0.0 copy-start.2
  3.4 0.9 %copy-done.2 = bf16[128,512]{1,0:T(8,128)(2,1)S(1)} copy-done((bf16[128,512]{1,0:T(8,128)(2,1)S(1)}, bf16[128,512]{1,0:T(8,128)(2,1)}, u32[]{:S(2)}) %copy-start.2) | copy-done | bytes 131096
  4.3 0.0 copy-start.4
  4.3 0.8 %copy-done.4 = bf16[128,128]{1,0:T(8,128)(2,1)S(1)} copy-done((bf16[128,128]{1,0:T(8,128)(2,1)S(1)}, bf16[128,128]{1,0:T(8,128)(2,1)}, u32[]{:S(2)}) %copy-start.4) | copy-done | bytes 32792
  5.1 42.8 %shard_map.131 = (bf16[16,32,128]{2,1,0:T(8,128)(2,1)S(1)}, bf16[16,32,128]{2,1,0:T(8,128)(2,1)S(1)}) custom-call(bf16[16,32,128]{2,1,0:T(8,128)(2,1)S(1)} %copy-done.1, f32[1,128]{1,0:T(1,128)S(1)} %bitcast.6, f32[1,128]{1,0:T(1,128)S(1)} %bitcast.7, bf16[128,640]{1,0:T(8,128)(2,1)S(1)} %copy-done, f32[1,128]{1,0:T(1,128)S(1)} %bitcast.8, ...), custom_call_target="tpu_custom_call" | custom-call | tf_op jit(solution)/shard_map/pallas_call | solution.py:271
  47.9 0.7 %copy.17 = bf16[16,32,128]{2,1,0:T(8,128)(2,1)} copy(bf16[16,32,128]{2,1,0:T(8,128)(2,1)S(1)} %get-tuple-element.4) | data formatting | bytes 262144
  48.6 0.7 %copy.18 = bf16[16,32,128]{2,1,0:T(8,128)(2,1)} copy(bf16[16,32,128]{2,1,0:T(8,128)(2,1)S(1)} %get-tuple-element.5) | data formatting | bytes 262144
Async XLA Ops:
  0.6 0.9 %copy-start.3 = (bf16[128,128]{1,0:T(8,128)(2,1)S(1)}, bf16[128,128]{1,0:T(8,128)(2,1)}, u32[]{:S(2)}) copy-start(bf16[128,128]{1,0:T(8,128)(2,1)} %tow_ref.1) | copy-start | bytes 98308
  0.6 0.9 %copy-start.5 = (f32[128]{0:T(128)S(1)}, f32[128]{0:T(128)}, u32[]{:S(2)}) copy-start(f32[128]{0:T(128)} %param.13) | copy-start | bytes 1540
  0.7 0.9 %copy-start.6 = (f32[128]{0:T(128)S(1)}, f32[128]{0:T(128)}, u32[]{:S(2)}) copy-start(f32[128]{0:T(128)} %param.14) | copy-start | bytes 1540
  0.7 0.9 %copy-start.7 = (f32[128]{0:T(128)S(1)}, f32[128]{0:T(128)}, u32[]{:S(2)}) copy-start(f32[128]{0:T(128)} %param.16) | copy-start | bytes 1540
  0.7 0.9 %copy-start.8 = (f32[128]{0:T(128)S(1)}, f32[128]{0:T(128)}, u32[]{:S(2)}) copy-start(f32[128]{0:T(128)} %param.17) | copy-start | bytes 1540
  0.7 0.9 %copy-start.9 = (f32[128]{0:T(128)S(1)}, f32[128]{0:T(128)}, u32[]{:S(2)}) copy-start(f32[128]{0:T(128)} %param.19) | copy-start | bytes 1540
  0.7 0.9 %copy-start.10 = (f32[128]{0:T(128)S(1)}, f32[128]{0:T(128)}, u32[]{:S(2)}) copy-start(f32[128]{0:T(128)} %param.20) | copy-start | bytes 1540
  1.6 0.9 %copy-start = (bf16[128,640]{1,0:T(8,128)(2,1)S(1)}, bf16[128,640]{1,0:T(8,128)(2,1)}, u32[]{:S(2)}) copy-start(bf16[128,640]{1,0:T(8,128)(2,1)} %tw_ref.1) | copy-start | bytes 491524
  2.5 0.9 %copy-start.1 = (bf16[16,32,128]{2,1,0:T(8,128)(2,1)S(1)}, bf16[16,32,128]{2,1,0:T(8,128)(2,1)}, u32[]{:S(2)}) copy-start(bf16[16,32,128]{2,1,0:T(8,128)(2,1)} %pair_ref.1) | copy-start | bytes 393220
  3.4 0.9 %copy-start.2 = (bf16[128,512]{1,0:T(8,128)(2,1)S(1)}, bf16[128,512]{1,0:T(8,128)(2,1)}, u32[]{:S(2)}) copy-start(bf16[128,512]{1,0:T(8,128)(2,1)} %aw_ref.1) | copy-start | bytes 393220
  4.3 0.8 %copy-start.4 = (bf16[128,128]{1,0:T(8,128)(2,1)S(1)}, bf16[128,128]{1,0:T(8,128)(2,1)}, u32[]{:S(2)}) copy-start(bf16[128,128]{1,0:T(8,128)(2,1)} %aow_ref.1) | copy-start | bytes 98308

commit v2 on v1

--- a/solution.py
+++ b/solution.py
@@ -30,15 +30,17 @@
 
 def kernel(
     R, C,
+    pair_hbm, ng_hbm, ns_hbm, tw_hbm, tg_hbm, ts_hbm, tow_hbm, ag_hbm, as_hbm, aw_hbm, bw_hbm, aow_hbm,
+    mid_ref, out_ref,
     pair_ref, ng_ref, ns_ref, tw_ref, tg_ref, ts_ref, tow_ref, ag_ref, as_ref, aw_ref, bw_ref, aow_ref,
-    mid_ref, out_ref,
+    fetch_sem,
     scr, gate_scr, send_a, recv_a, send_b, recv_b, send_d, recv_d, send_bias, recv_bias, send_f, recv_f,
     ssem_a, rsem_a, ssem_b, rsem_b, ssem_d, rsem_d, ssem_bias, rsem_bias, ssem_f, rsem_f,
 ):
     D = R * C
     rows, cols, width = pair_ref.shape
     hidden = tow_ref.shape[0]
-    heads = bw_ref.shape[1]
+    heads = bw_ref.shape[0]
     inner = aow_ref.shape[0]
     head_dim = inner // heads
     places = rows * cols
@@ -46,6 +48,7 @@
     per = hidden // D
     lanes = per * cols
     share = cols // R
+    parts, _, chunk = send_f.shape[:3]
     r, c = lax.axis_index("row"), lax.axis_index("col")
     me = r * C + c
 
@@ -59,6 +62,21 @@
         return _
 
     lax.fori_loop(1, D, greet, 0)
+
+    fetches = [
+        pltpu.make_async_copy(source, target, fetch_sem.at[n])
+        for n, (source, target) in enumerate(
+            [
+                (pair_hbm, pair_ref), (ng_hbm, ng_ref), (ns_hbm, ns_ref), (tw_hbm, tw_ref),
+                (tg_hbm, tg_ref), (ts_hbm, ts_ref), (tow_hbm, tow_ref), (ag_hbm, ag_ref),
+                (as_hbm, as_ref), (aw_hbm, aw_ref), (bw_hbm, bw_ref), (aow_hbm, aow_ref),
+            ]
+        )
+    ]
+    for fetch in fetches:
+        fetch.start()
+    for fetch in fetches[:4]:
+        fetch.wait()
 
     x = pair_ref[...].astype(f32).reshape(places, width)
     normed = normalize(x, ng_ref[...], ns_ref[...]).astype(bf16)
@@ -113,10 +131,10 @@
             device_id=(target, c), device_id_type=MESH,
         )
 
-    def copy_f(s, target, source):
-        return pltpu.make_async_remote_copy(
-            src_ref=send_f.at[target], dst_ref=recv_f.at[source],
-            send_sem=ssem_f.at[s], recv_sem=rsem_f.at[s],
+    def copy_f(part, s, target, source):
+        return pltpu.make_async_remote_copy(
+            src_ref=send_f.at[part, target], dst_ref=recv_f.at[part, source],
+            send_sem=ssem_f.at[part * R + s], recv_sem=rsem_f.at[part * R + s],
             device_id=(target, c), device_id_type=MESH,
         )
 
@@ -146,6 +164,8 @@
     gate_scr[...] = jax.nn.sigmoid(
         jnp.dot(normed, tw_ref[:, 4 * hidden :], preferred_element_type=f32)
     )
+    for fetch in fetches[4:]:
+        fetch.wait()
     arrive_all(copy_a, me, D)
 
     left = jnp.concatenate([recv_a[k, :, 0].reshape(residues, lanes) for k in range(C)], axis=1)
@@ -195,12 +215,13 @@
     wide = heads * cols
     spread_bw = jnp.concatenate(
         [
-            jnp.broadcast_to(bw_ref[:, h : h + 1].astype(f32), (width, cols))
+            jnp.broadcast_to(bw_ref[...].astype(f32)[h : h + 1], (cols, width))
             for h in range(heads)
         ],
-        axis=1,
+        axis=0,
     ).astype(bf16)
-    products = jnp.dot(att_t, spread_bw, preferred_element_type=f32).reshape(cols, rows, wide)
+    products = lax.dot_general(att_t, spread_bw, NT, preferred_element_type=f32)
+    products = products.reshape(cols, rows, wide)
     lane_col = lax.rem(lax.broadcasted_iota(jnp.int32, (rows, wide), 1), jnp.int32(cols))
     bias = jnp.zeros((rows, wide), f32)
     for y in range(cols):
@@ -238,22 +259,27 @@
                 part = part + full[h * cols : (h + 1) * cols]
             mixed.append(part)
         gated = (jnp.concatenate(mixed, axis=0) * gate).astype(bf16)
-        send_f[:, j] = gated.reshape(R, rows, inner)
-    start_all(copy_f, r, R)
-    recv_f[r] = send_f[r]
+        part, at = j // chunk, j % chunk
+        send_f[part, :, at] = gated.reshape(R, rows, inner)
+        if at == chunk - 1:
+            start_all(functools.partial(copy_f, part), r, R)
+            recv_f[part, r] = send_f[part, r]
     leave_all(copy_a, me, D)
     leave_all(copy_b, me, D)
     leave_all(copy_d, r, R)
     leave_all(copy_bias, me, D)
-    arrive_all(copy_f, r, R)
-    final = jnp.dot(
-        recv_f[...].reshape(places, inner), aow_ref[...], preferred_element_type=f32
-    )
-    for j in range(cols):
-        gate_scr[pl.ds(j, rows, stride=cols), :] = final[j * rows : (j + 1) * rows]
+    for part in range(parts):
+        arrive_all(functools.partial(copy_f, part), r, R)
+        final = jnp.dot(
+            recv_f[part].reshape(R * chunk * rows, inner), aow_ref[...], preferred_element_type=f32
+        )
+        for n in range(R * chunk):
+            j = n // chunk * share + part * chunk + n % chunk
+            gate_scr[pl.ds(j, rows, stride=cols), :] = final[n * rows : (n + 1) * rows]
     out = mid_ref[...].astype(f32).reshape(places, width) + gate_scr[...]
     out_ref[...] = out.astype(bf16).reshape(rows, cols, width)
-    leave_all(copy_f, r, R)
+    for part in range(parts):
+        leave_all(functools.partial(copy_f, part), r, R)
 
 
 def local(R, C, pair, ng, ns, tw, tg, ts, tow, ag, ash, aw, bw, aow):
@@ -261,6 +287,7 @@
     D = R * C
     hidden = tow.shape[0]
     heads = bw.shape[1]
+    parts = 2 if cols // R % 2 == 0 else 1
     inner = aow.shape[0]
     lanes = hidden // D * cols
     share = cols // R
@@ -268,34 +295,37 @@
     places = rows * cols
     vmem = pl.BlockSpec(memory_space=pltpu.VMEM)
     dma = pltpu.SemaphoreType.DMA
+    operands = (pair, ng[None], ns[None], tw, tg[None], ts[None], tow, ag[None], ash[None], aw, bw.T, aow)
     return pl.pallas_call(
         functools.partial(kernel, R, C),
         out_shape=(
             jax.ShapeDtypeStruct(pair.shape, bf16),
             jax.ShapeDtypeStruct(pair.shape, bf16),
         ),
-        in_specs=[vmem] * 12,
+        in_specs=[pl.BlockSpec(memory_space=pl.ANY)] * 12,
         out_specs=(vmem, vmem),
-        scratch_shapes=[
+        scratch_shapes=[pltpu.VMEM(v.shape, v.dtype) for v in operands]
+        + [
+            dma((12,)),
             pltpu.VMEM((D * rows, lanes), f32),
             pltpu.VMEM((places, width), f32),
             pltpu.VMEM((D, 2, rows, lanes), bf16),
             pltpu.VMEM((C, R, 2, rows, lanes), bf16),
-            pltpu.VMEM((C, R, rows, lanes), f32),
-            pltpu.VMEM((D, rows, lanes), f32),
+            pltpu.VMEM((C, R, rows, lanes), bf16),
+            pltpu.VMEM((D, rows, lanes), bf16),
             pltpu.VMEM((R, share, rows, width), bf16),
             pltpu.VMEM((R, share, rows, width), bf16),
             pltpu.VMEM((rows, wide), bf16),
             pltpu.VMEM((C, R, rows, wide), bf16),
-            pltpu.VMEM((R, share, rows, inner), bf16),
-            pltpu.VMEM((R, share, rows, inner), bf16),
+            pltpu.VMEM((parts, R, share // parts, rows, inner), bf16),
+            pltpu.VMEM((parts, R, share // parts, rows, inner), bf16),
             dma((D,)), dma((D,)), dma((D,)), dma((D,)), dma((R,)), dma((R,)),
-            dma((D,)), dma((D,)), dma((R,)), dma((R,)),
+            dma((D,)), dma((D,)), dma((parts * R,)), dma((parts * R,)),
         ],
         compiler_params=pltpu.CompilerParams(
-            collective_id=0, has_side_effects=True, vmem_limit_bytes=48 * 1024 * 1024
+            collective_id=0, has_side_effects=True, vmem_limit_bytes=63 * 1024 * 1024
         ),
-    )(pair, ng[None], ns[None], tw, tg[None], ts[None], tow, ag[None], ash[None], aw, bw, aow)
+    )(*operands)
 
 
 def solution(mesh):

time: 49.5 us -> 45.1 us (0.911)
  local copies, waits for them, and re-layouts: 5.67 us -> 2.26 us
  Pallas kernels: 42.8 us -> 42 us
    unnamed x25 -> x4, local copies, waits for them, and re-layouts: 5.67 us -> 2.26 us
    pallas_call x1, Pallas kernels: 42.8 us -> 42 us  [local(): pl.pallas_call(functools.partial(kernel, R, C), out_shape=(jax.ShapeDtype...]
where the time goes in v2:
time: 45.1 us; the launch traced here: 45 us
  Pallas kernels  42 us (93%)
  local copies, waits for them, and re-layouts  2.26 us (5%)
  between operations  0.65 us (1%)
    pallas_call x1, Pallas kernels, local(): pl.pallas_call(functools.partial(kernel, R, C), out_shape=(jax.ShapeDtype...  42 us
    unnamed x4, local copies, waits for them, and re-layouts  2.26 us

profile of v2, /device:TPU:0, one launch (start us, length us, event | category | flops | bytes accessed | tf_op | source)
XLA Modules:
  0.0 45.0 jit_solution(10088215962314836921)
XLA Ops:
  0.6 42.0 %shard_map.131 = (bf16[16,32,128]{2,1,0:T(8,128)(2,1)}, bf16[16,32,128]{2,1,0:T(8,128)(2,1)}) custom-call(bf16[16,32,128]{2,1,0:T(8,128)(2,1)} %pair_hbm.1, f32[1,128]{1,0:T(1,128)} %bitcast.8, f32[1,128]{1,0:T(1,128)} %bitcast.9, bf16[128,640]{1,0:T(8,128)(2,1)} %tw_hbm.1, f32[1,128]{1,0:T(1,128)} %bitcast.10, f32[1,128]{1,0:T(1,128)} %bitcast.11, ...), custom_call_target="tpu_custom_call" | custom-call | tf_op jit(solution)/shard_map/pallas_call | solution.py:299
  42.7 0.0 copy-start
  42.7 1.6 %copy.16 = bf16[16,32,128]{2,1,0:T(8,128)(2,1)} copy(bf16[16,32,128]{2,1,0:T(8,128)(2,1)} %get-tuple-element.4) | data formatting | bytes 262144
  44.3 0.0 copy-done
  44.3 0.7 %copy.17 = bf16[16,32,128]{2,1,0:T(8,128)(2,1)} copy(bf16[16,32,128]{2,1,0:T(8,128)(2,1)S(1)} %copy-done) | data formatting | bytes 262144
Async XLA Ops:
  42.7 1.6 %copy-start = (bf16[16,32,128]{2,1,0:T(8,128)(2,1)S(1)}, bf16[16,32,128]{2,1,0:T(8,128)(2,1)}, u32[]{:S(2)}) copy-start(bf16[16,32,128]{2,1,0:T(8,128)(2,1)} %get-tuple-element.5) | copy-start | bytes 393220

commit v3 on v2

--- a/solution.py
+++ b/solution.py
@@ -35,7 +35,7 @@
     pair_ref, ng_ref, ns_ref, tw_ref, tg_ref, ts_ref, tow_ref, ag_ref, as_ref, aw_ref, bw_ref, aow_ref,
     fetch_sem,
     scr, gate_scr, send_a, recv_a, send_b, recv_b, send_d, recv_d, send_bias, recv_bias, send_f, recv_f,
-    ssem_a, rsem_a, ssem_b, rsem_b, ssem_d, rsem_d, ssem_bias, rsem_bias, ssem_f, rsem_f,
+    sems,
 ):
     D = R * C
     rows, cols, width = pair_ref.shape
@@ -96,91 +96,64 @@
                 turned[h * D : (h + 1) * D, i * cols : (i + 1) * cols] for h in range(per)
             ]
             scr[pl.ds(i, D, stride=rows), :] = jnp.concatenate(pieces, axis=1)
-        send_a[:, side] = scr[...].astype(bf16).reshape(D, rows, lanes)
-
+        send_a[side] = scr[...].astype(bf16).reshape(D, rows, lanes)
+
+    def everywhere(source, target, send_sem, recv_sem):
+        def body(s, _):
+            t = lax.rem(me + s, D)
+            pltpu.make_async_remote_copy(
+                src_ref=source(t), dst_ref=target, send_sem=send_sem, recv_sem=recv_sem,
+                device_id=(lax.div(t, C), lax.rem(t, C)), device_id_type=MESH,
+            ).start()
+            return _
+
+        lax.fori_loop(1, D, body, 0)
+
+    def along_rows(source, target, send_sem, recv_sem):
+        def body(s, _):
+            t = lax.rem(r + s, R)
+            pltpu.make_async_remote_copy(
+                src_ref=source(t), dst_ref=target, send_sem=send_sem, recv_sem=recv_sem,
+                device_id=(t, c), device_id_type=MESH,
+            ).start()
+            return _
+
+        lax.fori_loop(1, R, body, 0)
+
+    def wait_bytes(ref, sem):
+        pltpu.make_async_copy(ref, ref, sem).wait()
+
+    spread_channels(1)
+    pl.semaphore_wait(barrier, D - 1)
+    everywhere(lambda t: send_a.at[1, t], recv_a.at[1, me], sems.at[0], sems.at[1])
     spread_channels(0)
-    spread_channels(1)
-
-    pl.semaphore_wait(barrier, D - 1)
-
-    def copy_a(s, target, source):
-        return pltpu.make_async_remote_copy(
-            src_ref=send_a.at[target], dst_ref=recv_a.at[lax.rem(source, C), lax.div(source, C)],
-            send_sem=ssem_a.at[s], recv_sem=rsem_a.at[s],
-            device_id=(lax.div(target, C), lax.rem(target, C)), device_id_type=MESH,
-        )
-
-    def copy_b(s, target, source):
-        return pltpu.make_async_remote_copy(
-            src_ref=send_b.at[lax.rem(target, C), lax.div(target, C)], dst_ref=recv_b.at[source],
-            send_sem=ssem_b.at[s], recv_sem=rsem_b.at[s],
-            device_id=(lax.div(target, C), lax.rem(target, C)), device_id_type=MESH,
-        )
-
-    def copy_bias(s, target, source):
-        return pltpu.make_async_remote_copy(
-            src_ref=send_bias, dst_ref=recv_bias.at[lax.rem(source, C), lax.div(source, C)],
-            send_sem=ssem_bias.at[s], recv_sem=rsem_bias.at[s],
-            device_id=(lax.div(target, C), lax.rem(target, C)), device_id_type=MESH,
-        )
-
-    def copy_d(s, target, source):
-        return pltpu.make_async_remote_copy(
-            src_ref=send_d.at[target], dst_ref=recv_d.at[source],
-            send_sem=ssem_d.at[s], recv_sem=rsem_d.at[s],
-            device_id=(target, c), device_id_type=MESH,
-        )
-
-    def copy_f(part, s, target, source):
-        return pltpu.make_async_remote_copy(
-            src_ref=send_f.at[part, target], dst_ref=recv_f.at[part, source],
-            send_sem=ssem_f.at[part * R + s], recv_sem=rsem_f.at[part * R + s],
-            device_id=(target, c), device_id_type=MESH,
-        )
-
-    def start_all(copy, here, count):
-        def body(s, _):
-            copy(s, lax.rem(here + s, count), here).start()
-            return _
-
-        lax.fori_loop(1, count, body, 0)
-
-    def arrive_all(copy, here, count):
-        def body(s, _):
-            copy(s, here, lax.rem(here + count - s, count)).wait_recv()
-            return _
-
-        lax.fori_loop(1, count, body, 0)
-
-    def leave_all(copy, here, count):
-        def body(s, _):
-            copy(s, lax.rem(here + s, count), here).wait_send()
-            return _
-
-        lax.fori_loop(1, count, body, 0)
-
-    start_all(copy_a, me, D)
-    recv_a[c, r] = send_a[me]
+    everywhere(lambda t: send_a.at[0, t], recv_a.at[0, me], sems.at[2], sems.at[3])
+    recv_a[0, me] = send_a[0, me]
+    recv_a[1, me] = send_a[1, me]
     gate_scr[...] = jax.nn.sigmoid(
         jnp.dot(normed, tw_ref[:, 4 * hidden :], preferred_element_type=f32)
     )
     for fetch in fetches[4:]:
         fetch.wait()
-    arrive_all(copy_a, me, D)
-
-    left = jnp.concatenate([recv_a[k, :, 0].reshape(residues, lanes) for k in range(C)], axis=1)
+    wait_bytes(recv_a.at[1, pl.ds(0, D - 1)], sems.at[1])
+    wait_bytes(recv_a.at[0, pl.ds(0, D - 1)], sems.at[3])
+
+    def arrived(side, k):
+        return jnp.concatenate([recv_a[side, q * C + k] for q in range(R)], axis=0)
+
+    left = jnp.concatenate([arrived(0, k) for k in range(C)], axis=1)
+    right = jnp.concatenate([arrived(1, k) for k in range(C)], axis=1)
     own_channel = jnp.concatenate([same_group(lanes, lanes, cols, cols)] * C, axis=1)
     for b in range(C):
-        block = jnp.concatenate(
-            [recv_a[k, :, 1].reshape(residues, lanes)[b * cols : (b + 1) * cols] for k in range(C)],
-            axis=1,
-        )
+        block = right[b * cols : (b + 1) * cols]
         block = jnp.where(own_channel, jnp.concatenate([block] * per, axis=0).astype(f32), 0.0)
         edges = lax.dot_general(left, block.astype(bf16), NT, preferred_element_type=f32)
         send_b[b] = edges.reshape(R, rows, lanes).astype(send_b.dtype)
-    start_all(copy_b, me, D)
+    everywhere(
+        lambda t: send_b.at[lax.rem(t, C), lax.div(t, C)], recv_b.at[me], sems.at[4], sems.at[5]
+    )
     recv_b[me] = send_b[c, r]
-    arrive_all(copy_b, me, D)
+    wait_bytes(recv_b.at[pl.ds(0, D - 1)], sems.at[5])
 
     def over_groups(v):
         total = v
@@ -211,7 +184,7 @@
         gate_scr[pl.ds(i, cols, stride=rows), :] = att_in[i * cols : (i + 1) * cols]
     att_t = gate_scr[...].astype(bf16)
     send_d[...] = att_t.reshape(R, share, rows, width)
-    start_all(copy_d, r, R)
+    along_rows(lambda t: send_d.at[t], recv_d.at[r], sems.at[6], sems.at[7])
     wide = heads * cols
     spread_bw = jnp.concatenate(
         [
@@ -227,15 +200,19 @@
     for y in range(cols):
         bias = jnp.where(lane_col == y, products[y], bias)
     send_bias[...] = bias.astype(bf16)
-    start_all(copy_bias, me, D)
+    everywhere(lambda t: send_bias, recv_bias.at[me], sems.at[8], sems.at[9])
     recv_d[r] = send_d[r]
-    recv_bias[c, r] = send_bias[...]
-    arrive_all(copy_d, r, R)
+    recv_bias[me] = send_bias[...]
+    wait_bytes(recv_d.at[pl.ds(0, R - 1)], sems.at[7])
 
     columns = [recv_d[:, j].reshape(residues, width) for j in range(share)]
     own_head = same_group(wide, inner, cols, head_dim)
     projected = [jnp.dot(a, aw_ref[...], preferred_element_type=f32) for a in columns]
-    arrive_all(copy_bias, me, D)
+    wait_bytes(recv_bias.at[pl.ds(0, D - 1)], sems.at[9])
+    biases = [
+        jnp.concatenate([recv_bias[q * C + b] for q in range(R)], axis=0).astype(f32)
+        for b in range(C)
+    ]
     for j in range(share):
         proj = projected[j]
         query = (proj[:, :inner] * head_dim ** (-0.5)).astype(bf16).astype(f32)
@@ -247,7 +224,7 @@
             tiled = jnp.concatenate([query[b * cols : (b + 1) * cols]] * heads, axis=0)
             tiled = jnp.where(own_head, tiled, 0.0).astype(bf16)
             scores = lax.dot_general(key, tiled, NT, preferred_element_type=f32)
-            scores = scores + recv_bias[b].reshape(residues, wide).astype(f32)
+            scores = scores + biases[b]
             top = jnp.max(scores, axis=0, keepdims=True)
             expd = jnp.exp(scores - top)
             total = jnp.sum(expd, axis=0, keepdims=True)
@@ -262,14 +239,13 @@
         part, at = j // chunk, j % chunk
         send_f[part, :, at] = gated.reshape(R, rows, inner)
         if at == chunk - 1:
-            start_all(functools.partial(copy_f, part), r, R)
+            along_rows(
+                lambda t, part=part: send_f.at[part, t], recv_f.at[part, r],
+                sems.at[10 + 2 * part], sems.at[11 + 2 * part],
+            )
             recv_f[part, r] = send_f[part, r]
-    leave_all(copy_a, me, D)
-    leave_all(copy_b, me, D)
-    leave_all(copy_d, r, R)
-    leave_all(copy_bias, me, D)
     for part in range(parts):
-        arrive_all(functools.partial(copy_f, part), r, R)
+        wait_bytes(recv_f.at[part, pl.ds(0, R - 1)], sems.at[11 + 2 * part])
         final = jnp.dot(
             recv_f[part].reshape(R * chunk * rows, inner), aow_ref[...], preferred_element_type=f32
         )
@@ -278,8 +254,13 @@
             gate_scr[pl.ds(j, rows, stride=cols), :] = final[n * rows : (n + 1) * rows]
     out = mid_ref[...].astype(f32).reshape(places, width) + gate_scr[...]
     out_ref[...] = out.astype(bf16).reshape(rows, cols, width)
+    wait_bytes(recv_a.at[1, pl.ds(0, D - 1)], sems.at[0])
+    wait_bytes(recv_a.at[0, pl.ds(0, D - 1)], sems.at[2])
+    wait_bytes(recv_b.at[pl.ds(0, D - 1)], sems.at[4])
+    wait_bytes(recv_d.at[pl.ds(0, R - 1)], sems.at[6])
+    wait_bytes(recv_bias.at[pl.ds(0, D - 1)], sems.at[8])
     for part in range(parts):
-        leave_all(functools.partial(copy_f, part), r, R)
+        wait_bytes(recv_f.at[part, pl.ds(0, R - 1)], sems.at[10 + 2 * part])
 
 
 def local(R, C, pair, ng, ns, tw, tg, ts, tow, ag, ash, aw, bw, aow):
@@ -309,18 +290,17 @@
             dma((12,)),
             pltpu.VMEM((D * rows, lanes), f32),
             pltpu.VMEM((places, width), f32),
-            pltpu.VMEM((D, 2, rows, lanes), bf16),
-            pltpu.VMEM((C, R, 2, rows, lanes), bf16),
+            pltpu.VMEM((2, D, rows, lanes), bf16),
+            pltpu.VMEM((2, D, rows, lanes), bf16),
             pltpu.VMEM((C, R, rows, lanes), bf16),
             pltpu.VMEM((D, rows, lanes), bf16),
             pltpu.VMEM((R, share, rows, width), bf16),
             pltpu.VMEM((R, share, rows, width), bf16),
             pltpu.VMEM((rows, wide), bf16),
-            pltpu.VMEM((C, R, rows, wide), bf16),
+            pltpu.VMEM((D, rows, wide), bf16),
             pltpu.VMEM((parts, R, share // parts, rows, inner), bf16),
             pltpu.VMEM((parts, R, share // parts, rows, inner), bf16),
-            dma((D,)), dma((D,)), dma((D,)), dma((D,)), dma((R,)), dma((R,)),
-            dma((D,)), dma((D,)), dma((parts * R,)), dma((parts * R,)),
+            dma((10 + 2 * parts,)),
         ],
         compiler_params=pltpu.CompilerParams(
             collective_id=0, has_side_effects=True, vmem_limit_bytes=63 * 1024 * 1024

time: 45.1 us -> 42.9 us (0.951)
  Pallas kernels: 42 us -> 39.8 us
    pallas_call x1, Pallas kernels: 42 us -> 39.8 us  [local(): pl.pallas_call(functools.partial(kernel, R, C), out_shape=(jax.ShapeDtype...]
where the time goes in v3:
time: 42.9 us; the launch traced here: 42.7 us
  Pallas kernels  39.8 us (93%)
  local copies, waits for them, and re-layouts  2.26 us (5%)
  between operations  0.65 us (2%)
    pallas_call x1, Pallas kernels, local(): pl.pallas_call(functools.partial(kernel, R, C), out_shape=(jax.ShapeDtype...  39.8 us
    unnamed x4, local copies, waits for them, and re-layouts  2.26 us

profile of v3, /device:TPU:0, one launch (start us, length us, event | category | flops | bytes accessed | tf_op | source)
XLA Modules:
  0.0 42.7 jit_solution(5770774806654709641)
XLA Ops:
  0.6 39.8 %shard_map.131 = (bf16[16,32,128]{2,1,0:T(8,128)(2,1)}, bf16[16,32,128]{2,1,0:T(8,128)(2,1)}) custom-call(bf16[16,32,128]{2,1,0:T(8,128)(2,1)} %pair_hbm.1, f32[1,128]{1,0:T(1,128)} %bitcast.8, f32[1,128]{1,0:T(1,128)} %bitcast.9, bf16[128,640]{1,0:T(8,128)(2,1)} %tw_hbm.1, f32[1,128]{1,0:T(1,128)} %bitcast.10, f32[1,128]{1,0:T(1,128)} %bitcast.11, ...), custom_call_target="tpu_custom_call" | custom-call | tf_op jit(solution)/shard_map/pallas_call | solution.py:280
  40.5 0.0 copy-start
  40.5 1.6 %copy.16 = bf16[16,32,128]{2,1,0:T(8,128)(2,1)} copy(bf16[16,32,128]{2,1,0:T(8,128)(2,1)} %get-tuple-element.4) | data formatting | bytes 262144
  42.1 0.0 copy-done
  42.1 0.7 %copy.17 = bf16[16,32,128]{2,1,0:T(8,128)(2,1)} copy(bf16[16,32,128]{2,1,0:T(8,128)(2,1)S(1)} %copy-done) | data formatting | bytes 262144
Async XLA Ops:
  40.5 1.6 %copy-start = (bf16[16,32,128]{2,1,0:T(8,128)(2,1)S(1)}, bf16[16,32,128]{2,1,0:T(8,128)(2,1)}, u32[]{:S(2)}) copy-start(bf16[16,32,128]{2,1,0:T(8,128)(2,1)} %get-tuple-element.5) | copy-start | bytes 393220

commit v4 on v3

--- a/solution.py
+++ b/solution.py
@@ -31,7 +31,7 @@
 def kernel(
     R, C,
     pair_hbm, ng_hbm, ns_hbm, tw_hbm, tg_hbm, ts_hbm, tow_hbm, ag_hbm, as_hbm, aw_hbm, bw_hbm, aow_hbm,
-    mid_ref, out_ref,
+    both_ref,
     pair_ref, ng_ref, ns_ref, tw_ref, tg_ref, ts_ref, tow_ref, ag_ref, as_ref, aw_ref, bw_ref, aow_ref,
     fetch_sem,
     scr, gate_scr, send_a, recv_a, send_b, recv_b, send_d, recv_d, send_bias, recv_bias, send_f, recv_f,
@@ -52,16 +52,8 @@
     r, c = lax.axis_index("row"), lax.axis_index("col")
     me = r * C + c
 
+    mid_ref, out_ref = both_ref.at[0], both_ref.at[1]
     barrier = pltpu.get_barrier_semaphore()
-
-    def greet(s, _):
-        t = lax.rem(me + s, D)
-        pl.semaphore_signal(
-            barrier, inc=1, device_id=(lax.div(t, C), lax.rem(t, C)), device_id_type=MESH
-        )
-        return _
-
-    lax.fori_loop(1, D, greet, 0)
 
     fetches = [
         pltpu.make_async_copy(source, target, fetch_sem.at[n])
@@ -75,11 +67,23 @@
     ]
     for fetch in fetches:
         fetch.start()
-    for fetch in fetches[:4]:
+
+    def greet(s, _):
+        t = lax.rem(me + s, D)
+        pl.semaphore_signal(
+            barrier, inc=1, device_id=(lax.div(t, C), lax.rem(t, C)), device_id_type=MESH
+        )
+        return _
+
+    lax.fori_loop(1, D, greet, 0)
+
+    for fetch in fetches[:3]:
         fetch.wait()
 
     x = pair_ref[...].astype(f32).reshape(places, width)
     normed = normalize(x, ng_ref[...], ns_ref[...]).astype(bf16)
+
+    fetches[3].wait()
 
     def spread_channels(side):
         at = 2 * hidden * side
@@ -184,7 +188,6 @@
         gate_scr[pl.ds(i, cols, stride=rows), :] = att_in[i * cols : (i + 1) * cols]
     att_t = gate_scr[...].astype(bf16)
     send_d[...] = att_t.reshape(R, share, rows, width)
-    along_rows(lambda t: send_d.at[t], recv_d.at[r], sems.at[6], sems.at[7])
     wide = heads * cols
     spread_bw = jnp.concatenate(
         [
@@ -200,29 +203,55 @@
     for y in range(cols):
         bias = jnp.where(lane_col == y, products[y], bias)
     send_bias[...] = bias.astype(bf16)
-    everywhere(lambda t: send_bias, recv_bias.at[me], sems.at[8], sems.at[9])
+    pairs = R // 2
+    pair_row, odd = lax.div(r, 2), lax.rem(r, 2)
+    slot = odd * C + c
+
+    def to_pairs(s, _):
+        t = lax.rem(pair_row + s, pairs)
+        pltpu.make_async_remote_copy(
+            src_ref=send_bias, dst_ref=recv_bias.at[slot, pair_row],
+            send_sem=sems.at[8], recv_sem=sems.at[9],
+            device_id=(t * 2 + odd, c), device_id_type=MESH,
+        ).start()
+        return _
+
+    def to_plane(s, _):
+        t = lax.rem(slot + s, 2 * C)
+        pltpu.make_async_remote_copy(
+            src_ref=recv_bias.at[slot], dst_ref=recv_bias.at[slot],
+            send_sem=sems.at[10 + 2 * parts], recv_sem=sems.at[11 + 2 * parts],
+            device_id=(pair_row * 2 + lax.div(t, C), lax.rem(t, C)), device_id_type=MESH,
+        ).start()
+        return _
+
+    lax.fori_loop(1, pairs, to_pairs, 0)
+    along_rows(lambda t: send_d.at[t], recv_d.at[r], sems.at[6], sems.at[7])
     recv_d[r] = send_d[r]
-    recv_bias[me] = send_bias[...]
+    recv_bias[slot, pair_row] = send_bias[...]
+    wait_bytes(recv_bias.at[0, pl.ds(0, pairs - 1)], sems.at[9])
+    lax.fori_loop(1, 2 * C, to_plane, 0)
     wait_bytes(recv_d.at[pl.ds(0, R - 1)], sems.at[7])
 
     columns = [recv_d[:, j].reshape(residues, width) for j in range(share)]
     own_head = same_group(wide, inner, cols, head_dim)
+    head_mask = jnp.where(own_head, 1.0, 0.0).astype(bf16)
     projected = [jnp.dot(a, aw_ref[...], preferred_element_type=f32) for a in columns]
-    wait_bytes(recv_bias.at[pl.ds(0, D - 1)], sems.at[9])
+    wait_bytes(recv_bias.at[pl.ds(0, 2 * C - 1)], sems.at[11 + 2 * parts])
     biases = [
-        jnp.concatenate([recv_bias[q * C + b] for q in range(R)], axis=0).astype(f32)
+        jnp.concatenate([recv_bias[q % 2 * C + b, q // 2] for q in range(R)], axis=0).astype(f32)
         for b in range(C)
     ]
     for j in range(share):
         proj = projected[j]
-        query = (proj[:, :inner] * head_dim ** (-0.5)).astype(bf16).astype(f32)
+        query = (proj[:, :inner] * head_dim ** (-0.5)).astype(bf16)
         key = proj[:, inner : 2 * inner].astype(bf16)
         value = proj[:, 2 * inner : 3 * inner].astype(bf16)
         gate = jax.nn.sigmoid(proj[:, 3 * inner :])
         mixed = []
         for b in range(C):
             tiled = jnp.concatenate([query[b * cols : (b + 1) * cols]] * heads, axis=0)
-            tiled = jnp.where(own_head, tiled, 0.0).astype(bf16)
+            tiled = tiled * head_mask
             scores = lax.dot_general(key, tiled, NT, preferred_element_type=f32)
             scores = scores + biases[b]
             top = jnp.max(scores, axis=0, keepdims=True)
@@ -258,7 +287,8 @@
     wait_bytes(recv_a.at[0, pl.ds(0, D - 1)], sems.at[2])
     wait_bytes(recv_b.at[pl.ds(0, D - 1)], sems.at[4])
     wait_bytes(recv_d.at[pl.ds(0, R - 1)], sems.at[6])
-    wait_bytes(recv_bias.at[pl.ds(0, D - 1)], sems.at[8])
+    wait_bytes(recv_bias.at[0, pl.ds(0, pairs - 1)], sems.at[8])
+    wait_bytes(recv_bias.at[pl.ds(0, 2 * C - 1)], sems.at[10 + 2 * parts])
     for part in range(parts):
         wait_bytes(recv_f.at[part, pl.ds(0, R - 1)], sems.at[10 + 2 * part])
 
@@ -277,14 +307,11 @@
     vmem = pl.BlockSpec(memory_space=pltpu.VMEM)
     dma = pltpu.SemaphoreType.DMA
     operands = (pair, ng[None], ns[None], tw, tg[None], ts[None], tow, ag[None], ash[None], aw, bw.T, aow)
-    return pl.pallas_call(
+    both = pl.pallas_call(
         functools.partial(kernel, R, C),
-        out_shape=(
-            jax.ShapeDtypeStruct(pair.shape, bf16),
-            jax.ShapeDtypeStruct(pair.shape, bf16),
-        ),
+        out_shape=jax.ShapeDtypeStruct((2, *pair.shape), bf16),
         in_specs=[pl.BlockSpec(memory_space=pl.ANY)] * 12,
-        out_specs=(vmem, vmem),
+        out_specs=vmem,
         scratch_shapes=[pltpu.VMEM(v.shape, v.dtype) for v in operands]
         + [
             dma((12,)),
@@ -297,15 +324,16 @@
             pltpu.VMEM((R, share, rows, width), bf16),
             pltpu.VMEM((R, share, rows, width), bf16),
             pltpu.VMEM((rows, wide), bf16),
-            pltpu.VMEM((D, rows, wide), bf16),
+            pltpu.VMEM((2 * C, R // 2, rows, wide), bf16),
             pltpu.VMEM((parts, R, share // parts, rows, inner), bf16),
             pltpu.VMEM((parts, R, share // parts, rows, inner), bf16),
-            dma((10 + 2 * parts,)),
+            dma((12 + 2 * parts,)),
         ],
         compiler_params=pltpu.CompilerParams(
             collective_id=0, has_side_effects=True, vmem_limit_bytes=63 * 1024 * 1024
         ),
     )(*operands)
+    return both[0], both[1]
 
 
 def solution(mesh):

time: 42.9 us -> 40.3 us (0.939)
  Pallas kernels: 39.8 us -> 37.9 us
  local copies, waits for them, and re-layouts: 2.26 us -> 1.69 us
    unnamed x4 -> x0, local copies, waits for them, and re-layouts: 2.26 us -> none
    pallas_call x1, Pallas kernels: 39.8 us -> 37.9 us  [local(): pl.pallas_call(functools.partial(kernel, R, C), out_shape=jax.ShapeDtypeS...]
    squeeze x0 -> x1, local copies, waits for them, and re-layouts: none -> 1.69 us  [local(): return (both[0], both[1])]
where the time goes in v4:
time: 40.3 us; the launch traced here: 40.2 us
  Pallas kernels  37.9 us (94%)
  local copies, waits for them, and re-layouts  1.69 us (4%)
  between operations  0.64 us (2%)
    pallas_call x1, Pallas kernels, local(): pl.pallas_call(functools.partial(kernel, R, C), out_shape=jax.ShapeDtypeS...  37.9 us
    squeeze x1, local copies, waits for them, and re-layouts, local(): return (both[0], both[1])  1.69 us

profile of v4, /device:TPU:0, one launch (start us, length us, event | category | flops | bytes accessed | tf_op | source)
XLA Modules:
  0.0 40.2 jit_solution(3817806292888067258)
XLA Ops:
  0.6 37.9 %shard_map.131 = bf16[2,16,32,128]{3,2,1,0:T(8,128)(2,1)} custom-call(bf16[16,32,128]{2,1,0:T(8,128)(2,1)} %pair_hbm.1, f32[1,128]{1,0:T(1,128)} %bitcast.12, f32[1,128]{1,0:T(1,128)} %bitcast.13, bf16[128,640]{1,0:T(8,128)(2,1)} %tw_hbm.1, f32[1,128]{1,0:T(1,128)} %bitcast.14, f32[1,128]{1,0:T(1,128)} %bitcast.15, bf16[128,128]{1,0:T(8,128)(2,1)} %tow_hbm.1, ...), custom_call_target="tpu_custom_call" | custom-call | tf_op jit(solution)/shard_map/pallas_call | solution.py:310
  38.5 1.7 %slice_bitcast_fusion = (bf16[16,32,128]{2,1,0:T(8,128)(2,1)}, bf16[16,32,128]{2,1,0:T(8,128)(2,1)}) fusion(bf16[2,16,32,128]{3,2,1,0:T(8,128)(2,1)} %shard_map.131), kind=kLoop, calls=%fused_computation | loop fusion | bytes 524288 | tf_op jit(solution)/shard_map/squeeze | solution.py:336
